TPU v7x, 128 devices: a whole 4x4x4 slice. The times are simulated.
128 devices in a mesh: frame: 16 (over z_lo, y, core), strip: 8 (over z_hi, x).
Axes of the slice: x: 4, y: 4, z: 4 (z_hi: 2, z_lo: 2; z = z_hi * 2 + z_lo), core: 2. Of those that a mesh axis runs over, the one named last changes fastest.
Arguments:
- latents: bfloat16 [32, 64, 128, 512], P('frame', None, 'strip'), may hold values from -29 to 38
- norm_first: float32 [2, 512], replicated, may hold values from -2 to 2, as said below
- conv_first: bfloat16 [3, 3, 512, 512], replicated, may hold values from -0.09375 to 0.09375
- bias_first: float32 [512], replicated, may hold values from -3 to 3
- norm_second: float32 [2, 512], replicated, may hold values from -2 to 2, as said below
- conv_second: bfloat16 [3, 3, 512, 512], replicated, may hold values from -0.09375 to 0.09375
- bias_second: float32 [512], replicated, may hold values from -3 to 3
- norm_third: float32 [2, 512], replicated, may hold values from -2 to 2, as said below
- time_first: bfloat16 [3, 512, 512], replicated, may hold values from -0.15625 to 0.15625
- tbias_first: float32 [512], replicated, may hold values from -3 to 3
- norm_fourth: float32 [2, 512], replicated, may hold values from -2 to 2, as said below
- time_second: bfloat16 [3, 512, 512], replicated, may hold values from -0.15625 to 0.15625
- tbias_second: float32 [512], replicated, may hold values from -3 to 3
- mix_factor: float32 [1], replicated, may hold values from -2 to 1
Outputs:
- mixed: bfloat16 [32, 64, 128, 512], P('frame', None, 'strip')
Inputs may be any that keep to these rules, and one draw needn't show every extreme that they name: `norm_first`: row 0 holds gains, row 1 shifts. `norm_second`: row 0 holds gains, row 1 shifts. `norm_third`: row 0 holds gains, row 1 shifts. `norm_fourth`: row 0 holds gains, row 1 shifts.
All inputs are finite; a program needn't handle non-finite values.
Results may differ from a plain program's by a relative error of at most 0.013.
Values may be sent and summed in bfloat16 or wider, within the bound.
A program may use at most 128 MiB of HBM per device.

v0:
```python
import jax
import jax.numpy as jnp
from jax import lax
from jax.sharding import PartitionSpec as P

GROUPS = 32


eps_norm = 1e-06


def with_halo(block, sides, width):
    for axis, dim in sides:
        count = lax.axis_size(axis)
        forward = [(i, i + 1) for i in range(count - 1)]
        backward = [(target, source) for source, target in forward]
        low = lax.ppermute(
            lax.slice_in_dim(block, block.shape[dim] - width, None, axis=dim), axis, forward
        )
        high = lax.ppermute(lax.slice_in_dim(block, 0, width, axis=dim), axis, backward)
        block = jnp.concatenate([low, block, high], axis=dim)
    return block


def group_total(per_channel):
    return per_channel.reshape(
        per_channel.shape[:-1] + (GROUPS, per_channel.shape[-1] // GROUPS)
    ).sum(-1)


def spread_channels(per_group, channels):
    return jnp.repeat(per_group, channels // GROUPS, axis=-1)


def frame_statistics(values):
    channels = values.shape[3]
    widened = values.astype(jnp.float32)
    members = values.shape[1] * values.shape[2] * lax.axis_size("strip") * (channels // GROUPS)
    average = lax.psum(group_total(jnp.sum(widened, axis=(1, 2))), "strip") / members
    centred = widened - spread_channels(average, channels)[:, None, None, :]
    variance = lax.psum(group_total(jnp.sum(centred * centred, axis=(1, 2))), "strip") / members
    return (
        spread_channels(average, channels)[:, None, None, :],
        spread_channels(lax.rsqrt(variance + eps_norm), channels)[:, None, None, :],
    )


def span_statistics(values):
    channels = values.shape[3]
    widened = values.astype(jnp.float32)
    members = (
        values.shape[0]
        * values.shape[1]
        * values.shape[2]
        * lax.axis_size("frame")
        * lax.axis_size("strip")
        * (channels // GROUPS)
    )
    average = lax.psum(group_total(jnp.sum(widened, axis=(0, 1, 2))), ("frame", "strip")) / members
    centred = widened - spread_channels(average, channels)
    variance = (
        lax.psum(group_total(jnp.sum(centred * centred, axis=(0, 1, 2))), ("frame", "strip"))
        / members
    )
    return (
        spread_channels(average, channels),
        spread_channels(lax.rsqrt(variance + eps_norm), channels),
    )


def normalize_act(values, params, moments):
    average, inverse = moments
    scaled = (values.astype(jnp.float32) - average) * inverse * params[0] + params[1]
    return jax.nn.silu(scaled).astype(jnp.bfloat16)


def spatial_conv(activation, kernel):
    widened = with_halo(activation, (("strip", 2),), 1)
    return lax.conv_general_dilated(
        widened,
        kernel,
        (1, 1),
        ((1, 1), (0, 0)),
        dimension_numbers=("NHWC", "HWIO", "NHWC"),
        preferred_element_type=jnp.float32,
    )


def temporal_conv(extended, weight):
    frames_here = extended.shape[0] - 2
    result = jnp.einsum(
        "frwc,cd->frwd", extended[0:frames_here], weight[0], preferred_element_type=jnp.float32
    )
    for offset in range(1, 3):
        result = result + jnp.einsum(
            "frwc,cd->frwd",
            extended[offset : offset + frames_here],
            weight[offset],
            preferred_element_type=jnp.float32,
        )
    return result


def frame_extend(activation):
    return with_halo(activation, (("frame", 0),), 1)


def temporal_block(
    spatial,
    extender,
    norm_third,
    time_first,
    tbias_first,
    norm_fourth,
    time_second,
    tbias_second,
    mix_factor,
):
    act_three = normalize_act(spatial, norm_third, span_statistics(spatial))
    tempo = (temporal_conv(extender(act_three), time_first) + tbias_first).astype(jnp.bfloat16)
    act_four = normalize_act(tempo, norm_fourth, span_statistics(tempo))
    branch = temporal_conv(extender(act_four), time_second) + tbias_second
    blend_factor = jax.nn.sigmoid(mix_factor[0])
    widened = spatial.astype(jnp.float32)
    return (blend_factor * widened + (1.0 - blend_factor) * (widened + branch)).astype(jnp.bfloat16)


def body(
    latents,
    norm_first,
    conv_first,
    bias_first,
    norm_second,
    conv_second,
    bias_second,
    norm_third,
    time_first,
    tbias_first,
    norm_fourth,
    time_second,
    tbias_second,
    mix_factor,
):
    act_one = normalize_act(latents, norm_first, frame_statistics(latents))
    first = (spatial_conv(act_one, conv_first) + bias_first).astype(jnp.bfloat16)
    act_two = normalize_act(first, norm_second, frame_statistics(first))
    second = spatial_conv(act_two, conv_second) + bias_second
    spatial = (latents.astype(jnp.float32) + second).astype(jnp.bfloat16)
    return temporal_block(
        spatial,
        frame_extend,
        norm_third,
        time_first,
        tbias_first,
        norm_fourth,
        time_second,
        tbias_second,
        mix_factor,
    )


def solution(mesh):
    placed = (
        P("frame", None, "strip", None),
        P(),
        P(),
        P(),
        P(),
        P(),
        P(),
        P(),
        P(),
        P(),
        P(),
        P(),
        P(),
        P(),
    )
    return jax.shard_map(
        body, mesh=mesh, in_specs=placed, out_specs=P("frame", None, "strip", None), check_vma=False
    )
```

profile of v0, /device:TPU:1, one launch (start us, length us, event | category | flops | bytes accessed | tf_op | source)
XLA Modules:
  0.0 524.4 jit_solution(13033311146915911323)
XLA Ops:
  0.0 2.2 convert_reduce_fusion.1
  2.4 22.1 %psum.56 = f32[2,32]{1,0:T(2,128)S(1)} all-reduce(f32[2,32]{1,0:T(2,128)S(1)} %reduce_sum.145), channel_id=1, replica_groups=mesh['frame'=16,'strip'=8] {'strip'}, use_global_device_ids=true, to_apply=%region_2.0 | all-reduce | flops 64 | bytes 512 | tf_op jit(solution)/shard_map/psum | solution.py:39
  24.6 2.2 fusion.27
  26.9 15.5 %psum.57 = f32[2,32]{1,0:T(2,128)S(1)} all-reduce(f32[2,32]{1,0:T(2,128)S(1)} %reduce_sum.147), channel_id=1, replica_groups=mesh['frame'=16,'strip'=8] {'strip'}, use_global_device_ids=true, to_apply=%region_5.0 | all-reduce | flops 64 | bytes 512 | tf_op jit(solution)/shard_map/psum | solution.py:41
  42.6 1.4 fusion.35
  44.5 3.4 collective-permute-start
  47.9 1.5 collective-permute-start.1
  49.4 1.8 collective-permute-done
  51.2 3.8 collective-permute-done.1
  55.0 2.2 maximum_bitcast_fusion
  60.8 16.6 %fusion.49 = f32[64,16,3,512]{3,1,2,0:T(8,128)S(1)} fusion(f32[512]{0:T(512)S(1)} %copy-done.14, pred[16,3]{0,1:T(4,128)(4,1)S(1)} %copy-done.16, bf16[3,3,512,512]{3,2,1,0:T(8,128)(2,1)S(1)} %bitcast.106, bf16[64,2,8,5,512]{4,0,3,2,1:T(8,128)(2,1)S(1)} %fusion.4), kind=kOutput, calls=%fused_computation.68 | convolution fusion | flops 14350811136 | bytes 16255024 | tf_op jit(solution)/shard_map/conv_general_dilated | solution.py:79
  77.4 3.6 copy.19
  81.5 15.7 %psum.58 = f32[2,32]{1,0:T(2,128)S(1)} all-reduce(f32[2,32]{1,0:T(2,128)S(1)} %reduce_sum.149), channel_id=1, replica_groups=mesh['frame'=16,'strip'=8] {'strip'}, use_global_device_ids=true, to_apply=%region_8.9 | all-reduce | flops 64 | bytes 512 | tf_op jit(solution)/shard_map/psum | solution.py:39
  98.2 4.2 copy-done.1
  102.4 6.9 %fusion.66 = f32[64,16,3,512]{3,1,2,0:T(8,128)} fusion(f32[64,16,3,512]{3,1,2,0:T(8,128)S(1)} %copy-done.1, f32[64,16,3,512]{3,0,2,1:T(8,128)S(1)} %bitcast.86), kind=kLoop, calls=%fused_computation.86 | loop fusion | flops 3145728 | bytes 18874368 | tf_op jit(solution)/shard_map/mul | solution.py:41
  109.4 6.4 %copy.21 = f32[64,16,3,512]{3,0,2,1:T(8,128)S(1)} copy(f32[64,16,3,512]{3,1,2,0:T(8,128)} %fusion.66) | data formatting | bytes 12582912 | tf_op jit(solution)/shard_map/mul | solution.py:41
  116.2 17.2 %psum.59 = f32[2,32]{1,0:T(2,128)S(1)} all-reduce(f32[2,32]{1,0:T(2,128)S(1)} %reduce_sum.151), channel_id=1, replica_groups=mesh['frame'=16,'strip'=8] {'strip'}, use_global_device_ids=true, to_apply=%region_11.12 | all-reduce | flops 64 | bytes 512 | tf_op jit(solution)/shard_map/psum | solution.py:41
  134.4 2.0 copy-done.3
  136.4 9.4 %multiply_convert_fusion = bf16[64,16,3,512]{3,1,2,0:T(8,128)(2,1)S(1)} fusion(f32[64,16,3,512]{3,0,2,1:T(8,128)S(1)} %bitcast.88, f32[512]{0:T(512)S(1)} %bitcast.100, f32[512]{0:T(512)S(1)} %bitcast.99, f32[64,16,3,512]{3,1,2,0:T(8,128)} %copy-done, f32[64,16,3,512]{3,0,2,1:T(8,128)S(1)} %bitcast.87), kind=kLoop, calls=%fused_computation.12 | loop fusion | flops 14155776 | bytes 22024192 | tf_op jit(solution)/shard_map/convert_element_type | solution.py:74
  145.8 1.8 copy.23
  147.7 1.6 collective-permute-start.2
  149.4 1.7 collective-permute-start.3
  151.3 5.6 %collective-permute-done.3 = bf16[2,64,1,512]{3,1,2,0:T(8,128)(2,1)S(1)} collective-permute-done((bf16[2,64,1,512]{3,1,2,0:T(8,128)(2,1)S(1)}, bf16[2,64,1,512]{3,1,2,0:T(8,128)(2,1)S(1)}, u32[]{:S(2)}, u32[]{:S(2)}) %collective-permute-start.3) | collective-permute-done | bytes 131104 | tf_op jit(solution)/shard_map/ppermute | solution.py:20
  159.9 16.4 %select_add_fusion = f32[64,16,3,512]{3,1,2,0:T(8,128)S(1)} fusion(f32[512]{0:T(512)S(1)} %copy-done.15, pred[16,3]{0,1:T(4,128)(4,1)S(1)} %copy-done.16, bf16[3,3,512,512]{3,2,1,0:T(8,128)(2,1)S(1)} %bitcast.108, bf16[64,2,8,5,512]{4,0,3,2,1:T(8,128)(2,1)S(1)} %fusion.5), kind=kOutput, calls=%fused_computation.11 | convolution fusion | flops 14347665408 | bytes 16255024 | tf_op jit(solution)/shard_map/conv_general_dilated | solution.py:79
  176.3 3.6 copy.25
  180.6 4.0 convert_reduce_fusion
  184.8 89.1 %psum.60 = f32[32]{0:T(128)S(1)} all-reduce(f32[32]{0:T(128)S(1)} %reduce_sum.153), channel_id=1, replica_groups=mesh['frame'=16,'strip'=8] {'frame','strip'}, use_global_device_ids=true, to_apply=%region_14.15 | all-reduce | flops 32 | bytes 256 | tf_op jit(solution)/shard_map/psum | solution.py:59
  274.0 2.2 fusion.18
  276.5 64.1 %psum.61 = f32[32]{0:T(128)S(1)} all-reduce(f32[32]{0:T(128)S(1)} %reduce_sum.155), channel_id=1, replica_groups=mesh['frame'=16,'strip'=8] {'frame','strip'}, use_global_device_ids=true, to_apply=%region_17.18 | all-reduce | flops 32 | bytes 256 | tf_op jit(solution)/shard_map/psum | solution.py:62
  340.7 3.2 fusion.26
  344.0 1.9 collective-permute-start.4
  346.0 2.5 collective-permute-start.5
  349.8 7.9 %collective-permute-done.4 = bf16[1,64,16,512]{3,2,1,0:T(8,128)(2,1)S(1)} collective-permute-done((bf16[1,64,16,512]{3,2,1,0:T(8,128)(2,1)S(1)}, bf16[1,64,16,512]{3,2,1,0:T(8,128)(2,1)S(1)}, u32[]{:S(2)}, u32[]{:S(2)}) %collective-permute-start.4) | collective-permute-done | bytes 1048608 | tf_op jit(solution)/shard_map/ppermute | solution.py:17
  357.7 1.3 fusion.50
  359.0 3.1 collective-permute-done.5
  362.1 3.0 convert_reduce_fusion.2
  365.3 66.1 %psum.62 = f32[32]{0:T(128)S(1)} all-reduce(f32[32]{0:T(128)S(1)} %reduce_sum.157), channel_id=1, replica_groups=mesh['frame'=16,'strip'=8] {'frame','strip'}, use_global_device_ids=true, to_apply=%region_20.21 | all-reduce | flops 32 | bytes 256 | tf_op jit(solution)/shard_map/psum | solution.py:59
  431.6 2.2 fusion.36
  434.0 64.1 %psum.63 = f32[32]{0:T(128)S(1)} all-reduce(f32[32]{0:T(128)S(1)} %reduce_sum.159), channel_id=1, replica_groups=mesh['frame'=16,'strip'=8] {'frame','strip'}, use_global_device_ids=true, to_apply=%region_23.24 | all-reduce | flops 32 | bytes 256 | tf_op jit(solution)/shard_map/psum | solution.py:62
  498.3 3.0 fusion.44
  501.3 1.5 fusion.94
  502.8 1.9 collective-permute-start.6
  504.7 3.6 collective-permute-start.7
  509.1 2.4 fusion.76
  511.6 5.2 collective-permute-done.6
  516.8 2.5 fusion.58
  519.3 1.8 collective-permute-done.7
  521.1 3.1 fusion.47
  (105 shorter events, 14.5 us)
Async XLA Ops:
  0.0 42.6 %copy-start.4 = (bf16[2,64,16,512]{3,2,1,0:T(8,128)(2,1)S(1)}, bf16[2,64,16,512]{3,2,1,0:T(8,128)(2,1)}, u32[]{:S(2)}) copy-start(bf16[2,64,16,512]{3,2,1,0:T(8,128)(2,1)} %param.14) | copy-start | bytes 6291460
  0.0 42.6 %copy-start.10 = (f32[2,512]{1,0:T(2,128)S(1)}, f32[2,512]{1,0:T(2,128)}, u32[]{:S(2)}) copy-start(f32[2,512]{1,0:T(2,128)} %param.15) | copy-start | bytes 12292
  2.2 47.2 %copy-start.11 = (f32[2,512]{1,0:T(2,128)S(1)}, f32[2,512]{1,0:T(2,128)}, u32[]{:S(2)}) copy-start(f32[2,512]{1,0:T(2,128)} %param.18) | copy-start | bytes 12292
  44.5 6.7 %collective-permute-start = (bf16[2,64,1,512]{3,2,1,0:T(2,128)(2,1)S(1)}, bf16[2,64,1,512]{3,2,1,0:T(2,128)(2,1)S(1)}, u32[]{:S(2)}, u32[]{:S(2)}) collective-permute-start(bf16[2,64,1,512]{3,2,1,0:T(2,128)(2,1)S(1)} %get-tuple-element.13), channel_id=1, source_target_pairs={{0,1},{1,2},{2,3},{3,4},{4,5},{5,6},{6,7},{8,9},{9,10},{10,11},{11... | collective-permute-start | bytes 393224 | tf_op jit(solution)/shard_map/ppermute | solution.py:17
  47.9 7.1 %collective-permute-start.1 = (bf16[2,64,1,512]{3,2,1,0:T(2,128)(2,1)S(1)}, bf16[2,64,1,512]{3,2,1,0:T(2,128)(2,1)S(1)}, u32[]{:S(2)}, u32[]{:S(2)}) collective-permute-start(bf16[2,64,1,512]{3,2,1,0:T(2,128)(2,1)S(1)} %get-tuple-element.14), channel_id=1, source_target_pairs={{1,0},{2,1},{3,2},{4,3},{5,4},{6,5},{7,6},{9,8},{10,9},{11,10},{12... | collective-permute-start | bytes 393224 | tf_op jit(solution)/shard_map/ppermute | solution.py:20
  58.5 2.2 slice-start
  58.7 2.1 slice-start.1
  58.7 2.1 copy-start.14
  58.7 2.1 copy-start.16
  77.4 3.7 copy-start
  97.4 5.1 copy-start.1
  98.2 11.2 %copy-start.2 = (f32[64,2,24,512]{3,0,2,1:T(8,128)}, f32[64,2,24,512]{3,0,2,1:T(8,128)S(1)}, u32[]{:S(2)}) copy-start(f32[64,2,24,512]{3,0,2,1:T(8,128)S(1)} %broadcast.36) | copy-start | bytes 18874372
  133.6 2.8 copy-start.3
  147.7 3.6 collective-permute-start.2
  149.4 7.5 %collective-permute-start.3 = (bf16[2,64,1,512]{3,1,2,0:T(8,128)(2,1)S(1)}, bf16[2,64,1,512]{3,1,2,0:T(8,128)(2,1)S(1)}, u32[]{:S(2)}, u32[]{:S(2)}) collective-permute-start(bf16[2,64,1,512]{3,1,2,0:T(8,128)(2,1)S(1)} %get-tuple-element.12), channel_id=1, source_target_pairs={{1,0},{2,1},{3,2},{4,3},{5,4},{6,5},{7,6},{9,8},{10,9},{11,10},{12... | collective-permute-start | bytes 393224 | tf_op jit(solution)/shard_map/ppermute | solution.py:20
  157.5 2.2 slice-start.2
  157.7 2.1 slice-start.3
  157.7 2.1 copy-start.15
  180.6 95.8 %copy-start.12 = (f32[2,512]{1,0:T(2,128)S(1)}, f32[2,512]{1,0:T(2,128)}, u32[]{:S(2)}) copy-start(f32[2,512]{1,0:T(2,128)} %param.21) | copy-start | bytes 12292
  340.7 7.7 %copy-start.6 = (bf16[3,512,512]{2,1,0:T(8,128)(2,1)S(1)}, bf16[3,512,512]{2,1,0:T(8,128)(2,1)}, u32[]{:S(2)}) copy-start(bf16[3,512,512]{2,1,0:T(8,128)(2,1)} %param.22) | copy-start | bytes 4718596
  344.0 13.7 %collective-permute-start.4 = (bf16[1,64,16,512]{3,2,1,0:T(8,128)(2,1)S(1)}, bf16[1,64,16,512]{3,2,1,0:T(8,128)(2,1)S(1)}, u32[]{:S(2)}, u32[]{:S(2)}) collective-permute-start(bf16[1,64,16,512]{3,2,1,0:T(8,128)(2,1)S(1)} %get-tuple-element.10), channel_id=1, source_target_pairs={{0,8},{8,16},{16,24},{24,32},{32,40},{40,48},{48,56},{56,64},{64,7... | collective-permute-start | bytes 3145736 | tf_op jit(solution)/shard_map/ppermute | solution.py:17
  346.0 16.1 %collective-permute-start.5 = (bf16[1,64,16,512]{3,2,1,0:T(8,128)(2,1)S(1)}, bf16[1,64,16,512]{3,2,1,0:T(8,128)(2,1)S(1)}, u32[]{:S(2)}, u32[]{:S(2)}) collective-permute-start(bf16[1,64,16,512]{3,2,1,0:T(8,128)(2,1)S(1)} %get-tuple-element.9), channel_id=1, source_target_pairs={{8,0},{16,8},{24,16},{32,24},{40,32},{48,40},{56,48},{64,56},{72,6... | collective-permute-start | bytes 3145736 | tf_op jit(solution)/shard_map/ppermute | solution.py:20
  349.7 12.4 %copy-start.8 = (f32[512]{0:T(512)S(1)}, f32[512]{0:T(512)}, u32[]{:S(2)}) copy-start(f32[512]{0:T(512)} %param.23) | copy-start | bytes 6148
  359.0 75.0 %copy-start.13 = (f32[2,512]{1,0:T(2,128)S(1)}, f32[2,512]{1,0:T(2,128)}, u32[]{:S(2)}) copy-start(f32[2,512]{1,0:T(2,128)} %param.24) | copy-start | bytes 12292
  502.8 14.0 %collective-permute-start.6 = (bf16[1,64,16,512]{3,2,1,0:T(8,128)(2,1)}, bf16[1,64,16,512]{3,2,1,0:T(8,128)(2,1)}, u32[]{:S(2)}, u32[]{:S(2)}) collective-permute-start(bf16[1,64,16,512]{3,2,1,0:T(8,128)(2,1)} %get-tuple-element.8), channel_id=1, source_target_pairs={{0,8},{8,16},{16,24},{24,32},{32,40},{40,48},{48,56},{56,64},{64,7... | collective-permute-start | bytes 3145736 | tf_op jit(solution)/shard_map/ppermute | solution.py:17
  504.7 16.3 %collective-permute-start.7 = (bf16[1,64,16,512]{3,2,1,0:T(8,128)(2,1)}, bf16[1,64,16,512]{3,2,1,0:T(8,128)(2,1)S(1)}, u32[]{:S(2)}, u32[]{:S(2)}) collective-permute-start(bf16[1,64,16,512]{3,2,1,0:T(8,128)(2,1)} %get-tuple-element.7), channel_id=1, source_target_pairs={{8,0},{16,8},{24,16},{32,24},{40,32},{48,40},{56,48},{64,56},{72,6... | collective-permute-start | bytes 3145736 | tf_op jit(solution)/shard_map/ppermute | solution.py:20
  509.1 7.7 %copy-start.7 = (bf16[3,512,512]{2,1,0:T(8,128)(2,1)S(1)}, bf16[3,512,512]{2,1,0:T(8,128)(2,1)}, u32[]{:S(2)}) copy-start(bf16[3,512,512]{2,1,0:T(8,128)(2,1)} %param.25) | copy-start | bytes 4718596
  511.5 9.5 %copy-start.5 = (bf16[2,64,16,512]{3,2,1,0:T(8,128)(2,1)S(1)}, bf16[2,64,16,512]{3,2,1,0:T(8,128)(2,1)}, u32[]{:S(2)}) copy-start(bf16[2,64,16,512]{3,2,1,0:T(8,128)(2,1)} %get-tuple-element.6) | copy-start | bytes 6291460
  511.6 9.5 %copy-start.9 = (f32[512]{0:T(512)S(1)}, f32[512]{0:T(512)}, u32[]{:S(2)}) copy-start(f32[512]{0:T(512)} %param.26) | copy-start | bytes 6148
where the time goes:
time: 530 us; the launch traced here: 524 us
  blocking collectives  354 us (67%)
  matrix products  46.6 us (9%)
  other arithmetic  42.2 us (8%)
  local copies, waits for them, and re-layouts  32.9 us (6%)
  waiting for transfers between devices  29.4 us (6%)
  starting transfers between devices  18.1 us (3%)
    psum x2, blocking collectives, span_statistics(): lax.psum(group_total(jnp.sum(widened, axis=(0, 1, 2))), ('frame', 'strip'))  155 us
    psum x2, blocking collectives, span_statistics(): lax.psum(group_total(jnp.sum(centred * centred, axis=(0, 1, 2))), ('frame...  128 us
    psum x2, blocking collectives, frame_statistics(): lax.psum(group_total(jnp.sum(widened, axis=(1, 2))), 'strip') / members  37.7 us
    conv_general_dilated x2, matrix products, spatial_conv(): lax.conv_general_dilated(widened, kernel, (1, 1), ((1, 1), (0, 0)), dimen...  33 us
    psum x2, blocking collectives, frame_statistics(): lax.psum(group_total(jnp.sum(centred * centred, axis=(1, 2))), 'strip')  32.7 us
    convert_element_type x4, other arithmetic, normalize_act(): return jax.nn.silu(scaled).astype(jnp.bfloat16)  17 us
    ppermute x4, waiting for transfers between devices, with_halo(): lax.ppermute(lax.slice_in_dim(block, block.shape[dim] - width, None, axis...  15.2 us
    ppermute x4, waiting for transfers between devices, with_halo(): lax.ppermute(lax.slice_in_dim(block, 0, width, axis=dim), axis, backward)  14.2 us
  transfers between devices with their start and end apart: 8, of which 8 were waited for; matrix products, arithmetic and copies ran while one was open for 1% of the time, Pallas kernels for 0%

commit v1 on v0

v1 whole, which is shorter than its diff:
```python
import functools

import jax
import jax.numpy as jnp
from jax import lax
from jax.experimental import pallas as pl
from jax.experimental.pallas import tpu as pltpu
from jax.sharding import PartitionSpec as P

MESH = pl.DeviceIdType.MESH
F32 = jnp.float32
BF16 = jnp.bfloat16
C = 512
ROWS = 64
COLS = 16
PAIRS = COLS // 2
POS = ROWS * COLS
GROUP = 16
HALF = 256
EPS = 1e-06


def drain(ref, sem):
    pltpu.make_async_copy(ref, ref, sem).wait()


def combine(tiles, count):
    n = tiles.shape[0]
    means, squares = tiles[:, 0:4, :], tiles[:, 4:8, :]
    mean = jnp.sum(means, axis=0) * (1.0 / n)
    gap = means - mean[None]
    return mean, jnp.sum(squares, axis=0) + count * jnp.sum(gap * gap, axis=0)


def row_of(tile):
    return jnp.concatenate([tile[q : q + 1, :] for q in range(4)], axis=1)


def coefficients(mean, square, count, group_sum, params):
    eight = jnp.concatenate([mean, mean], axis=0)
    centre = jnp.dot(eight, group_sum, preferred_element_type=F32, precision=lax.Precision.HIGHEST)
    centre = centre[0:4] * (1.0 / GROUP)
    gap = mean - centre
    total = square + count * gap * gap
    total = jnp.concatenate([total, total], axis=0)
    spread = jnp.dot(total, group_sum, preferred_element_type=F32, precision=lax.Precision.HIGHEST)
    inverse = lax.rsqrt(spread[0:4] * (1.0 / (GROUP * count)) + EPS)
    return row_of(centre), 0.5 * row_of(inverse) * params[0:1, :], 0.5 * params[1:2, :]


def act(values, coef):
    mean, scale, shift = coef
    h = (values.astype(F32) - mean) * scale + shift
    return h + h * jnp.tanh(h)


def put_moments(tile_ref, lo, mean, square):
    for q in range(mean.shape[1] // 128):
        at = lo // 128 + q
        tile_ref[at : at + 1, :] = mean[:, q * 128 : (q + 1) * 128]
        tile_ref[at + 4 : at + 5, :] = square[:, q * 128 : (q + 1) * 128]


def kernel(
    nf,
    ns,
    lat_hbm,
    norm1,
    conv1_hbm,
    bias1,
    norm2,
    conv2_hbm,
    bias2,
    norm3,
    time1_hbm,
    tbias1,
    norm4,
    time2_hbm,
    tbias2,
    mix,
    out_hbm,
    raw,
    lx,
    halo1,
    u1,
    u2,
    tw1,
    tw2,
    s,
    v,
    fx,
    halo2,
    sp,
    near,
    far,
    dd,
    a3,
    tm,
    td,
    perm,
    st_own,
    st1,
    st2,
    st3s,
    st3f,
    st4s,
    st4f,
    load_sem,
    u1_sem,
    u2_sem,
    tw_sem,
    halo_send,
    halo_recv,
    stat_send,
    stat_recv,
    frame_send,
    frame_recv,
    out_sem,
):
    f = lax.axis_index("frame")
    st = lax.axis_index("strip")
    core = lax.rem(f, 2)
    first_frame = core
    second_frame = 1 - core
    partner = f + 1 - 2 * core
    has_peer = jnp.logical_and(f > 0, f < nf - 1)
    peer = jnp.where(has_peer, f - 1 + 2 * core, partner)
    has_left, has_right = st > 0, st < ns - 1

    barrier = pltpu.get_barrier_semaphore()
    for d in range(1, ns):
        pl.semaphore_signal(barrier, inc=1, device_id={"strip": lax.rem(st + d, ns)}, device_id_type=MESH)
    for d in range(1, nf):
        pl.semaphore_signal(barrier, inc=1, device_id={"frame": lax.rem(f + d, nf)}, device_id_type=MESH)

    load = pltpu.make_async_copy(lat_hbm, raw, load_sem)
    load.start()

    def conv_loads(hbm, u, sem):
        copies = []
        for j, slot in ((0, 0), (1, 2), (2, 3)):
            for i in range(3):
                copies.append(
                    pltpu.make_async_copy(hbm.at[i, j], u.at[slot, pl.ds(i * C, C), :], sem.at[slot, i])
                )
        for copy in copies:
            copy.start()
        return copies

    u1_loads = conv_loads(conv1_hbm, u1, u1_sem)
    u2_loads = conv_loads(conv2_hbm, u2, u2_sem)
    tw_loads = []
    for n, (hbm, tw) in enumerate(((time1_hbm, tw1), (time2_hbm, tw2))):
        for k in range(3):
            tap = k + core * (2 - 2 * k)
            tw_loads.append(pltpu.make_async_copy(hbm.at[tap], tw.at[pl.ds(k * C, C), :], tw_sem.at[n, k]))
    for copy in tw_loads:
        copy.start()

    i0 = lax.broadcasted_iota(jnp.int32, (HALF, HALF), 0)
    i1 = lax.broadcasted_iota(jnp.int32, (HALF, HALF), 1)
    perm[...] = jnp.where(i1 == (i0 & 15) * 16 + (i0 >> 4), 1.0, 0.0).astype(BF16)
    g0 = lax.broadcasted_iota(jnp.int32, (128, 128), 0)
    g1 = lax.broadcasted_iota(jnp.int32, (128, 128), 1)
    group_sum = jnp.where((g0 >> 4) == (g1 >> 4), 1.0, 0.0).astype(F32)

    s[:, 0:8, :] = jnp.zeros((COLS + 2, 8, C), F32)
    s[:, 72:80, :] = jnp.zeros((COLS + 2, 8, C), F32)

    load.wait()

    @pl.loop(0, 8)
    def _(n):
        fr, b = n // 4, lax.rem(n, 4)
        block = raw[fr, pl.ds(b * HALF, HALF), :]
        moved = jnp.dot(perm[...], block, preferred_element_type=F32)
        lx[fr, :, :, pl.ds(pl.multiple_of(b * 16, 16), 16), :] = moved.reshape(PAIRS, 2, 16, C).astype(BF16)

    for fr in range(2):
        zero = jnp.zeros((8, C), F32)

        def add_up(c, total, fr=fr):
            return total + jnp.sum(lx[fr, c // 2, lax.rem(c, 2)].astype(F32).reshape(8, 8, C), axis=0)

        mean = jnp.sum(lax.fori_loop(0, COLS, add_up, zero), axis=0, keepdims=True) * (1.0 / POS)

        def add_squares(c, total, fr=fr, mean=mean):
            gap = lx[fr, c // 2, lax.rem(c, 2)].astype(F32) - mean
            return total + jnp.sum((gap * gap).reshape(8, 8, C), axis=0)

        square = jnp.sum(lax.fori_loop(0, COLS, add_squares, zero), axis=0, keepdims=True)
        put_moments(st_own.at[fr], 0, mean, square)

    def transform_weights(u):
        @pl.loop(0, 3 * C // 32)
        def _(n):
            at = pl.ds(pl.multiple_of(n * 32, 32), 32)
            outer = (u[0, at, :].astype(F32) + u[3, at, :].astype(F32)) * 0.5
            middle = u[2, at, :].astype(F32) * 0.5
            u[1, at, :] = (outer + middle).astype(BF16)
            u[2, at, :] = (outer - middle).astype(BF16)

    for copy in u1_loads:
        copy.wait()
    transform_weights(u1)

    pl.semaphore_wait(barrier, ns - 1 + nf - 1)

    def strip_gather(src, slots, k):
        for d in range(1, ns):
            pltpu.make_async_remote_copy(
                src, slots.at[d - 1], stat_send.at[k], stat_recv.at[k],
                device_id={"strip": lax.rem(st + d, ns)}, device_id_type=MESH,
            ).start()

    def frame_gather(src, slots, k):
        for d in range(1, nf):
            pltpu.make_async_remote_copy(
                src, slots.at[d - 1], stat_send.at[k], stat_recv.at[k],
                device_id={"frame": lax.rem(f + d, nf)}, device_id_type=MESH,
            ).start()

    def gather_wait(slots, k):
        drain(slots, stat_recv.at[k])
        drain(slots, stat_send.at[k])

    def edge_copies(x, halo, fr, order, k):
        to_left = pltpu.make_async_remote_copy(
            x.at[fr, 0, 0], halo.at[order, 1], halo_send.at[k, 0], halo_recv.at[k, 1],
            device_id={"strip": lax.max(st - 1, 0)}, device_id_type=MESH,
        )
        to_right = pltpu.make_async_remote_copy(
            x.at[fr, PAIRS - 1, 1], halo.at[order, 0], halo_send.at[k, 1], halo_recv.at[k, 0],
            device_id={"strip": lax.min(st + 1, ns - 1)}, device_id_type=MESH,
        )
        return to_left, to_right

    def edges_start(x, halo, fr, order, k):
        to_left, to_right = edge_copies(x, halo, fr, order, k)
        pl.when(has_left)(lambda: to_left.start())
        pl.when(has_right)(lambda: to_right.start())

    def edges_wait(x, halo, fr, order, k):
        to_left, to_right = edge_copies(x, halo, fr, order, k)

        @pl.when(has_left)
        def _():
            to_left.wait_send()
            to_right.wait_recv()

        @pl.when(has_right)
        def _():
            to_right.wait_send()
            to_left.wait_recv()

        @pl.when(jnp.logical_not(has_left))
        def _():
            halo[order, 0] = jnp.zeros((ROWS, C), BF16)

        @pl.when(jnp.logical_not(has_right))
        def _():
            halo[order, 1] = jnp.zeros((ROWS, C), BF16)

    for order, fr in ((0, first_frame), (1, second_frame)):
        edges_start(lx, halo1, fr, order, order)
    strip_gather(st_own.at[pl.ds(0, 2)], st1, 0)

    for copy in u2_loads:
        copy.wait()
    transform_weights(u2)

    gather_wait(st1, 0)

    def spatial_stage(x, halo, fr, order, coef, u, finish):
        @pl.loop(0, COLS)
        def _(c):
            s[c + 1, 8:72, :] = act(x[fr, c // 2, lax.rem(c, 2)], coef)

        s[0, 8:72, :] = jnp.where(has_left, act(halo[order, 0], coef), 0.0)
        s[COLS + 1, 8:72, :] = jnp.where(has_right, act(halo[order, 1], coef), 0.0)

        @pl.loop(0, PAIRS)
        def _(p):
            rows = pl.ds(pl.multiple_of(p * ROWS, ROWS), ROWS)
            for i in range(3):
                for q in range(4):
                    lanes = slice(q * 128, (q + 1) * 128)
                    d = [s[2 * p + k, 7 + i : 71 + i, lanes] for k in range(4)]
                    to = slice(i * C + q * 128, i * C + (q + 1) * 128)
                    v[0, rows, to] = (d[0] - d[2]).astype(BF16)
                    v[1, rows, to] = (d[1] + d[2]).astype(BF16)
                    v[2, rows, to] = (d[2] - d[1]).astype(BF16)
                    v[3, rows, to] = (d[1] - d[3]).astype(BF16)

        for n in range(2):
            lanes = slice(n * HALF, (n + 1) * HALF)
            m = [
                jnp.concatenate(
                    [jnp.dot(v[t, h * HALF : (h + 1) * HALF], u[t, :, lanes], preferred_element_type=F32) for h in range(2)],
                    axis=0,
                )
                for t in range(4)
            ]
            finish(n, lanes, m[0] + m[1] + m[2], m[1] - m[2] - m[3])

    def moments_of(parts):
        count = sum(part.shape[0] for part in parts)
        mean = sum(jnp.sum(part, axis=0, keepdims=True) for part in parts) * (1.0 / count)
        square = sum(jnp.sum((part - mean) * (part - mean), axis=0, keepdims=True) for part in parts)
        return mean, square

    for order, fr in ((0, first_frame), (1, second_frame)):
        tiles = jnp.concatenate([st1[:, fr], st_own[fr][None]], axis=0)
        mean, square = combine(tiles, float(POS))
        coef = coefficients(mean, square, float(POS * ns), group_sum, norm1)
        edges_wait(lx, halo1, fr, order, order)

        def finish(n, lanes, even, odd, fr=fr, order=order):
            even, odd = even + bias1[:, lanes], odd + bias1[:, lanes]
            fx[fr, :, 0, :, lanes] = even.reshape(PAIRS, ROWS, HALF).astype(BF16)
            fx[fr, :, 1, :, lanes] = odd.reshape(PAIRS, ROWS, HALF).astype(BF16)
            put_moments(st_own.at[2 + order], n * HALF, *moments_of([even, odd]))

        spatial_stage(lx, halo1, fr, order, coef, u1, finish)
        edges_start(fx, halo2, fr, order, 2 + order)
        strip_gather(st_own.at[2 + order], st2.at[order], 1 + order)

    def to_peer(order, n, lanes):
        dst = near if order == 0 else far
        fr = first_frame if order == 0 else second_frame
        return pltpu.make_async_remote_copy(
            sp.at[fr, :, :, :, lanes], dst.at[:, :, :, lanes], frame_send.at[order, n], frame_recv.at[order, n],
            device_id={"frame": peer}, device_id_type=MESH,
        )

    def to_partner(n, lanes):
        return pltpu.make_async_remote_copy(
            sp.at[second_frame, :, :, :, lanes], dd.at[:, :, :, lanes], frame_send.at[2, n], frame_recv.at[2, n],
            device_id={"frame": partner}, device_id_type=MESH,
        )

    for order, fr in ((0, first_frame), (1, second_frame)):
        gather_wait(st2.at[order], 1 + order)
        tiles = jnp.concatenate([st2[order], st_own[2 + order][None]], axis=0)
        mean, square = combine(tiles, float(POS))
        coef = coefficients(mean, square, float(POS * ns), group_sum, norm2)
        edges_wait(fx, halo2, fr, order, 2 + order)

        def finish(n, lanes, even, odd, fr=fr, order=order):
            parts = []
            for k, part in enumerate((even, odd)):
                old = lx[fr, :, k, :, lanes].astype(F32).reshape(PAIRS * ROWS, HALF)
                part = (part + bias2[:, lanes]) + old
                sp[fr, :, k, :, lanes] = part.reshape(PAIRS, ROWS, HALF).astype(BF16)
                parts.append(part)
            put_moments(st_own.at[4 + order], n * HALF, *moments_of(parts))
            pl.when(has_peer)(lambda: to_peer(order, n, lanes).start())
            if order == 1:
                to_partner(n, lanes).start()

        spatial_stage(fx, halo2, fr, order, coef, u2, finish)

    def span_first(lo, slot, k, slots):
        mean, square = combine(st_own[lo : lo + 2], float(POS))
        st_own[slot] = jnp.concatenate([mean, square], axis=0)
        strip_gather(st_own.at[slot], slots, k)

    def span_second(slot, k, slots, out_slot, out_k, out_slots):
        gather_wait(slots, k)
        mean, square = combine(jnp.concatenate([slots[...], st_own[slot][None]], axis=0), float(2 * POS))
        st_own[out_slot] = jnp.concatenate([mean, square], axis=0)
        frame_gather(st_own.at[out_slot], out_slots, out_k)

    def span_done(slot, k, slots, params):
        gather_wait(slots, k)
        mean, square = combine(jnp.concatenate([slots[...], st_own[slot][None]], axis=0), float(2 * POS * ns))
        return coefficients(mean, square, float(2 * POS * ns * nf), group_sum, params)

    span_first(4, 6, 3, st3s)
    span_second(6, 3, st3s, 7, 4, st3f)
    coef3 = span_done(7, 4, st3f, norm3)

    def fill(dst, src, coef):
        @pl.loop(0, COLS)
        def _(c):
            dst[pl.ds(pl.multiple_of(c * ROWS, ROWS), ROWS), :] = act(src[c // 2, lax.rem(c, 2)], coef).astype(BF16)

    fill(a3.at[2], sp.at[first_frame], coef3)
    fill(a3.at[3], sp.at[second_frame], coef3)
    for copy in tw_loads:
        copy.wait()

    def temporal(at, tw, lanes):
        taps = jnp.concatenate([a3[at - 1], a3[at], a3[at + 1]], axis=1)
        return jnp.dot(taps, tw[:, lanes], preferred_element_type=F32)

    for n in range(2):
        lanes = slice(n * HALF, (n + 1) * HALF)
        copy = to_partner(n, lanes)
        copy.wait_send()
        copy.wait_recv()
    fill(a3.at[4], dd, coef3)

    def tempo_frame(order, moments):
        for n in range(2):
            lanes = slice(n * HALF, (n + 1) * HALF)
            values = temporal(1 + order, tw1, lanes) + tbias1[:, lanes]
            tm[order, :, :, :, lanes] = values.reshape(PAIRS, 2, ROWS, HALF).astype(BF16)
            if moments:
                put_moments(st_own.at[7 + order], n * HALF, *moments_of([values]))

    tempo_frame(2, True)
    tempo_copy = pltpu.make_async_remote_copy(
        tm.at[2], td, frame_send.at[3, 0], frame_recv.at[3, 0], device_id={"frame": partner}, device_id_type=MESH
    )
    tempo_copy.start()

    def peer_wait(order):
        @pl.when(has_peer)
        def _():
            for n in range(2):
                copy = to_peer(order, n, slice(n * HALF, (n + 1) * HALF))
                copy.wait_send()
                copy.wait_recv()

    def fill_or_zero(dst, src, coef):
        pl.when(has_peer)(lambda: fill(dst, src, coef))

        @pl.when(jnp.logical_not(has_peer))
        def _():
            @pl.loop(0, COLS)
            def _(c):
                dst[pl.ds(pl.multiple_of(c * ROWS, ROWS), ROWS), :] = jnp.zeros((ROWS, C), BF16)

    peer_wait(0)
    fill_or_zero(a3.at[1], near, coef3)
    tempo_frame(1, True)
    span_first(8, 10, 5, st4s)
    span_second(10, 5, st4s, 11, 6, st4f)

    peer_wait(1)
    fill_or_zero(a3.at[0], far, coef3)
    tempo_frame(0, False)

    coef4 = span_done(11, 6, st4f, norm4)
    fill(a3.at[2], tm.at[1], coef4)
    fill(a3.at[3], tm.at[2], coef4)
    fill_or_zero(a3.at[1], tm.at[0], coef4)
    tempo_copy.wait_send()
    tempo_copy.wait_recv()
    fill(a3.at[4], td, coef4)

    keep = 1.0 - 1.0 / (1.0 + jnp.exp(-jnp.full((1, HALF), mix[0], F32)))
    out_copies = []
    for order, fr in ((0, first_frame), (1, second_frame)):
        for n in range(2):
            lanes = slice(n * HALF, (n + 1) * HALF)
            branch = temporal(2 + order, tw2, lanes) + tbias2[:, lanes]
            old = sp[fr, :, :, :, lanes].astype(F32).reshape(POS, HALF)
            lx[fr, :, :, :, lanes] = (old + keep * branch).reshape(PAIRS, 2, ROWS, HALF).astype(BF16)

        @pl.loop(0, 4)
        def _(b, fr=fr):
            block = lx[fr, :, :, pl.ds(pl.multiple_of(b * 16, 16), 16), :].reshape(HALF, C)
            moved = jnp.dot(perm[...], block, preferred_element_type=F32)
            raw[fr, pl.ds(pl.multiple_of(b * HALF, HALF), HALF), :] = moved.astype(BF16)

        copy = pltpu.make_async_copy(raw.at[fr], out_hbm.at[fr], out_sem.at[order])
        copy.start()
        out_copies.append(copy)
    for copy in out_copies:
        copy.wait()


def body(*args):
    nf, ns = lax.axis_size("frame"), lax.axis_size("strip")
    (
        latents, norm1, conv1, bias1, norm2, conv2, bias2, norm3, time1, tbias1, norm4, time2, tbias2, mix,
    ) = args
    vmem = pl.BlockSpec(memory_space=pltpu.VMEM)
    hbm = pl.BlockSpec(memory_space=pl.ANY)
    smem = pl.BlockSpec(memory_space=pltpu.SMEM)
    tile = (8, 128)
    frame = (PAIRS, 2, ROWS, C)
    out = pl.pallas_call(
        functools.partial(kernel, nf, ns),
        out_shape=jax.ShapeDtypeStruct((2, POS, C), BF16),
        in_specs=[hbm, vmem, hbm, vmem, vmem, hbm, vmem, vmem, hbm, vmem, vmem, hbm, vmem, smem],
        out_specs=hbm,
        scratch_shapes=[
            pltpu.VMEM((2, POS, C), BF16),
            pltpu.VMEM((2,) + frame, BF16),
            pltpu.VMEM((2, 2, ROWS, C), BF16),
            pltpu.VMEM((4, 3 * C, C), BF16),
            pltpu.VMEM((4, 3 * C, C), BF16),
            pltpu.VMEM((3 * C, C), BF16),
            pltpu.VMEM((3 * C, C), BF16),
            pltpu.VMEM((COLS + 2, 80, C), F32),
            pltpu.VMEM((4, PAIRS * ROWS, 3 * C), BF16),
            pltpu.VMEM((2,) + frame, BF16),
            pltpu.VMEM((2, 2, ROWS, C), BF16),
            pltpu.VMEM((2,) + frame, BF16),
            pltpu.VMEM(frame, BF16),
            pltpu.VMEM(frame, BF16),
            pltpu.VMEM(frame, BF16),
            pltpu.VMEM((5, POS, C), BF16),
            pltpu.VMEM((3,) + frame, BF16),
            pltpu.VMEM(frame, BF16),
            pltpu.VMEM((HALF, HALF), BF16),
            pltpu.VMEM((12,) + tile, F32),
            pltpu.VMEM((ns - 1, 2) + tile, F32),
            pltpu.VMEM((2, ns - 1) + tile, F32),
            pltpu.VMEM((ns - 1,) + tile, F32),
            pltpu.VMEM((nf - 1,) + tile, F32),
            pltpu.VMEM((ns - 1,) + tile, F32),
            pltpu.VMEM((nf - 1,) + tile, F32),
            pltpu.SemaphoreType.DMA,
            pltpu.SemaphoreType.DMA((4, 3)),
            pltpu.SemaphoreType.DMA((4, 3)),
            pltpu.SemaphoreType.DMA((2, 3)),
            pltpu.SemaphoreType.DMA((4, 2)),
            pltpu.SemaphoreType.DMA((4, 2)),
            pltpu.SemaphoreType.DMA((7,)),
            pltpu.SemaphoreType.DMA((7,)),
            pltpu.SemaphoreType.DMA((4, 2)),
            pltpu.SemaphoreType.DMA((4, 2)),
            pltpu.SemaphoreType.DMA((2,)),
        ],
        compiler_params=pltpu.CompilerParams(
            collective_id=0, has_side_effects=True, vmem_limit_bytes=62 * 2**20
        ),
        cost_estimate=pl.CostEstimate(flops=20 * 10**9, bytes_accessed=17 * 2**20, transcendentals=8 * 10**6),
    )(
        latents.reshape(2, POS, C),
        norm1,
        conv1,
        bias1.reshape(1, C),
        norm2,
        conv2,
        bias2.reshape(1, C),
        norm3,
        time1,
        tbias1.reshape(1, C),
        norm4,
        time2,
        tbias2.reshape(1, C),
        mix,
    )
    return out.reshape(2, ROWS, COLS, C)


def solution(mesh):
    placed = (P("frame", None, "strip", None),) + (P(),) * 13
    return jax.shard_map(
        body, mesh=mesh, in_specs=placed, out_specs=P("frame", None, "strip", None), check_vma=False
    )
```

time: 530 us -> 102 us (0.19); the launches traced: 524 us -> 102 us
  blocking collectives: 354 us -> 0 us
  Pallas kernels: 0 us -> 98.3 us
  matrix products: 46.6 us -> 0 us
  other arithmetic: 42.2 us -> 0 us
  local copies, waits for them, and re-layouts: 32.9 us -> 3.08 us
  waiting for transfers between devices: 29.4 us -> 0 us
  starting transfers between devices: 18.1 us -> 0 us
    psum x8 -> x0, blocking collectives: 354 us -> none  [the longest x2 155 us: span_statistics(): lax.psum(group_total(jnp.sum(widened, axis=(0, 1, 2))), ('frame', 'strip'))]
    pallas_call x0 -> x1, Pallas kernels: none -> 98.3 us  [body(): pl.pallas_call(functools.partial(kernel, nf, ns), out_shape=jax.ShapeDtyp...]
    conv_general_dilated x2 -> x0, matrix products: 33 us -> none  [spatial_conv(): lax.conv_general_dilated(widened, kernel, (1, 1), ((1, 1), (0, 0)), dimen...]
    ppermute x8 -> x0, waiting for transfers between devices: 29.4 us -> none  [the longest x4 15.2 us: with_halo(): lax.ppermute(lax.slice_in_dim(block, block.shape[dim] - width, None, axis...]
    ppermute x8 -> x0, starting transfers between devices: 18.1 us -> none  [the longest x4 9.26 us: with_halo(): lax.ppermute(lax.slice_in_dim(block, 0, width, axis=dim), axis, backward)]
    convert_element_type x4 -> x0, other arithmetic: 17 us -> none  [normalize_act(): return jax.nn.silu(scaled).astype(jnp.bfloat16)]
    reduce_sum x15 -> x0, other arithmetic: 14.1 us -> none  [the longest x2 4.42 us: span_statistics(): jnp.sum(centred * centred, axis=(0, 1, 2))]
    dot_general x6 -> x0, matrix products: 13.6 us -> none  [the longest x4 9.82 us: temporal_conv(): jnp.einsum('frwc,cd->frwd', extended[offset:offset + frames_here], weight...]
  transfers between devices with their start and end apart: 8 -> 0, of which waited for: 8 -> 0; matrix products, arithmetic and copies ran while one was open for 1% -> 0% of each run, Pallas kernels for 0% -> 0%
where the time goes in v1:
time: 102 us
  Pallas kernels  98.3 us (96%)
  local copies, waits for them, and re-layouts  3.08 us (3%)
    pallas_call x1, Pallas kernels, body(): pl.pallas_call(functools.partial(kernel, nf, ns), out_shape=jax.ShapeDtyp...  98.3 us
    unnamed x1, local copies, waits for them, and re-layouts  3.08 us

profile of v1, /device:TPU:1, one launch (start us, length us, event | category | flops | bytes accessed | tf_op | source)
XLA Modules:
  0.0 102.1 jit_solution(16707583370287813170)
XLA Ops:
  0.7 98.3 %shard_map.136 = bf16[2,1024,512]{2,1,0:T(8,128)(2,1)} custom-call(bf16[2,1024,512]{2,1,0:T(8,128)(2,1)} %bitcast.7, f32[2,512]{1,0:T(2,128)} %norm1.1, bf16[3,3,512,512]{3,2,1,0:T(8,128)(2,1)} %conv1_hbm.1, f32[1,512]{1,0:T(1,128)} %bitcast.8, f32[2,512]{1,0:T(2,128)} %norm2.1, bf16[3,3,512,512]{3,2,1,0:T(8,128)(2,1)} %conv2_hbm.1, f32[1,512]{1,0:T(1,128)} %bitcast.9, ...), custom_call_target="tpu_custom_call" | custom-call | flops 20000000000 | bytes 17825792 | tf_op jit(solution)/shard_map/pallas_call | solution.py:485
  99.0 3.1 %copy.17 = bf16[2,64,16,512]{3,2,1,0:T(8,128)(2,1)} copy(bf16[2,64,16,512]{3,2,1,0:T(8,128)(2,1)} %bitcast.6) | data formatting | bytes 4194304

commit v2 on v1

--- a/solution.py
+++ b/solution.py
@@ -157,24 +157,18 @@
     for copy in tw_loads:
         copy.start()
 
-    i0 = lax.broadcasted_iota(jnp.int32, (HALF, HALF), 0)
-    i1 = lax.broadcasted_iota(jnp.int32, (HALF, HALF), 1)
-    perm[...] = jnp.where(i1 == (i0 & 15) * 16 + (i0 >> 4), 1.0, 0.0).astype(BF16)
+    perm[...] = transposition()
     g0 = lax.broadcasted_iota(jnp.int32, (128, 128), 0)
     g1 = lax.broadcasted_iota(jnp.int32, (128, 128), 1)
     group_sum = jnp.where((g0 >> 4) == (g1 >> 4), 1.0, 0.0).astype(F32)
 
-    s[:, 0:8, :] = jnp.zeros((COLS + 2, 8, C), F32)
-    s[:, 72:80, :] = jnp.zeros((COLS + 2, 8, C), F32)
-
     load.wait()
 
-    @pl.loop(0, 8)
-    def _(n):
-        fr, b = n // 4, lax.rem(n, 4)
-        block = raw[fr, pl.ds(b * HALF, HALF), :]
+    for n in range(8):
+        fr, b = n // 4, n % 4
+        block = raw[fr, b * HALF : (b + 1) * HALF, :]
         moved = jnp.dot(perm[...], block, preferred_element_type=F32)
-        lx[fr, :, :, pl.ds(pl.multiple_of(b * 16, 16), 16), :] = moved.reshape(PAIRS, 2, 16, C).astype(BF16)
+        lx[fr, :, :, b * 16 : (b + 1) * 16, :] = moved.reshape(PAIRS, 2, 16, C).astype(BF16)
 
     for fr in range(2):
         zero = jnp.zeros((8, C), F32)
@@ -261,9 +255,8 @@
         def _():
             halo[order, 1] = jnp.zeros((ROWS, C), BF16)
 
-    for order, fr in ((0, first_frame), (1, second_frame)):
-        edges_start(lx, halo1, fr, order, order)
     strip_gather(st_own.at[pl.ds(0, 2)], st1, 0)
+    edges_start(lx, halo1, first_frame, 0, 0)
 
     for copy in u2_loads:
         copy.wait()
@@ -272,25 +265,27 @@
     gather_wait(st1, 0)
 
     def spatial_stage(x, halo, fr, order, coef, u, finish):
-        @pl.loop(0, COLS)
+        @pl.loop(0, COLS, unroll=4)
         def _(c):
-            s[c + 1, 8:72, :] = act(x[fr, c // 2, lax.rem(c, 2)], coef)
-
-        s[0, 8:72, :] = jnp.where(has_left, act(halo[order, 0], coef), 0.0)
-        s[COLS + 1, 8:72, :] = jnp.where(has_right, act(halo[order, 1], coef), 0.0)
+            s[c + 1] = act(x[fr, c // 2, lax.rem(c, 2)], coef)
+
+        s[0] = jnp.where(has_left, act(halo[order, 0], coef), 0.0)
+        s[COLS + 1] = jnp.where(has_right, act(halo[order, 1], coef), 0.0)
 
         @pl.loop(0, PAIRS)
         def _(p):
             rows = pl.ds(pl.multiple_of(p * ROWS, ROWS), ROWS)
-            for i in range(3):
-                for q in range(4):
-                    lanes = slice(q * 128, (q + 1) * 128)
-                    d = [s[2 * p + k, 7 + i : 71 + i, lanes] for k in range(4)]
-                    to = slice(i * C + q * 128, i * C + (q + 1) * 128)
-                    v[0, rows, to] = (d[0] - d[2]).astype(BF16)
-                    v[1, rows, to] = (d[1] + d[2]).astype(BF16)
-                    v[2, rows, to] = (d[2] - d[1]).astype(BF16)
-                    v[3, rows, to] = (d[1] - d[3]).astype(BF16)
+            top = lax.broadcasted_iota(jnp.int32, (ROWS, 128), 0) == 0
+            bottom = lax.broadcasted_iota(jnp.int32, (ROWS, 128), 0) == ROWS - 1
+            for q in range(4):
+                lo = q * 128
+                d = [s[2 * p + k, :, lo : lo + 128] for k in range(4)]
+                for t, part in enumerate((d[0] - d[2], d[1] + d[2], d[2] - d[1], d[1] - d[3])):
+                    above = jnp.where(top, 0.0, pltpu.roll(part, 1, 0))
+                    below = jnp.where(bottom, 0.0, pltpu.roll(part, ROWS - 1, 0))
+                    v[t, rows, lo : lo + 128] = above.astype(BF16)
+                    v[t, rows, C + lo : C + lo + 128] = part.astype(BF16)
+                    v[t, rows, 2 * C + lo : 2 * C + lo + 128] = below.astype(BF16)
 
         for n in range(2):
             lanes = slice(n * HALF, (n + 1) * HALF)
@@ -314,6 +309,8 @@
         mean, square = combine(tiles, float(POS))
         coef = coefficients(mean, square, float(POS * ns), group_sum, norm1)
         edges_wait(lx, halo1, fr, order, order)
+        if order == 0:
+            edges_start(lx, halo1, second_frame, 1, 1)
 
         def finish(n, lanes, even, odd, fr=fr, order=order):
             even, odd = even + bias1[:, lanes], odd + bias1[:, lanes]
@@ -322,8 +319,8 @@
             put_moments(st_own.at[2 + order], n * HALF, *moments_of([even, odd]))
 
         spatial_stage(lx, halo1, fr, order, coef, u1, finish)
+        strip_gather(st_own.at[2 + order], st2.at[order], 1 + order)
         edges_start(fx, halo2, fr, order, 2 + order)
-        strip_gather(st_own.at[2 + order], st2.at[order], 1 + order)
 
     def to_peer(order, n, lanes):
         dst = near if order == 0 else far
@@ -354,7 +351,8 @@
                 sp[fr, :, k, :, lanes] = part.reshape(PAIRS, ROWS, HALF).astype(BF16)
                 parts.append(part)
             put_moments(st_own.at[4 + order], n * HALF, *moments_of(parts))
-            pl.when(has_peer)(lambda: to_peer(order, n, lanes).start())
+            if order == 0:
+                pl.when(has_peer)(lambda: to_peer(0, n, lanes).start())
             if order == 1:
                 to_partner(n, lanes).start()
 
@@ -380,8 +378,13 @@
     span_second(6, 3, st3s, 7, 4, st3f)
     coef3 = span_done(7, 4, st3f, norm3)
 
+    @pl.when(has_peer)
+    def _():
+        for n in range(2):
+            to_peer(1, n, slice(n * HALF, (n + 1) * HALF)).start()
+
     def fill(dst, src, coef):
-        @pl.loop(0, COLS)
+        @pl.loop(0, COLS, unroll=4)
         def _(c):
             dst[pl.ds(pl.multiple_of(c * ROWS, ROWS), ROWS), :] = act(src[c // 2, lax.rem(c, 2)], coef).astype(BF16)
 
@@ -391,8 +394,12 @@
         copy.wait()
 
     def temporal(at, tw, lanes):
-        taps = jnp.concatenate([a3[at - 1], a3[at], a3[at + 1]], axis=1)
-        return jnp.dot(taps, tw[:, lanes], preferred_element_type=F32)
+        parts = []
+        for h in range(POS // HALF):
+            rows = slice(h * HALF, (h + 1) * HALF)
+            taps = jnp.concatenate([a3[at - 1, rows], a3[at, rows], a3[at + 1, rows]], axis=1)
+            parts.append(jnp.dot(taps, tw[:, lanes], preferred_element_type=F32))
+        return jnp.concatenate(parts, axis=0)
 
     for n in range(2):
         lanes = slice(n * HALF, (n + 1) * HALF)
@@ -459,17 +466,22 @@
             old = sp[fr, :, :, :, lanes].astype(F32).reshape(POS, HALF)
             lx[fr, :, :, :, lanes] = (old + keep * branch).reshape(PAIRS, 2, ROWS, HALF).astype(BF16)
 
-        @pl.loop(0, 4)
-        def _(b, fr=fr):
-            block = lx[fr, :, :, pl.ds(pl.multiple_of(b * 16, 16), 16), :].reshape(HALF, C)
-            moved = jnp.dot(perm[...], block, preferred_element_type=F32)
-            raw[fr, pl.ds(pl.multiple_of(b * HALF, HALF), HALF), :] = moved.astype(BF16)
-
-        copy = pltpu.make_async_copy(raw.at[fr], out_hbm.at[fr], out_sem.at[order])
+        copy = pltpu.make_async_copy(lx.at[fr], out_hbm.at[fr], out_sem.at[order])
         copy.start()
         out_copies.append(copy)
     for copy in out_copies:
         copy.wait()
+
+
+def transposition():
+    i0 = lax.broadcasted_iota(jnp.int32, (HALF, HALF), 0)
+    i1 = lax.broadcasted_iota(jnp.int32, (HALF, HALF), 1)
+    return jnp.where(i1 == (i0 & 15) * 16 + (i0 >> 4), 1.0, 0.0).astype(BF16)
+
+
+def untransposed(x, out):
+    moved = jnp.dot(transposition(), x[0].reshape(HALF, C), preferred_element_type=F32)
+    out[0] = moved.astype(BF16)
 
 
 def body(*args):
@@ -484,7 +496,7 @@
     frame = (PAIRS, 2, ROWS, C)
     out = pl.pallas_call(
         functools.partial(kernel, nf, ns),
-        out_shape=jax.ShapeDtypeStruct((2, POS, C), BF16),
+        out_shape=jax.ShapeDtypeStruct((2,) + frame, BF16),
         in_specs=[hbm, vmem, hbm, vmem, vmem, hbm, vmem, vmem, hbm, vmem, vmem, hbm, vmem, smem],
         out_specs=hbm,
         scratch_shapes=[
@@ -495,7 +507,7 @@
             pltpu.VMEM((4, 3 * C, C), BF16),
             pltpu.VMEM((3 * C, C), BF16),
             pltpu.VMEM((3 * C, C), BF16),
-            pltpu.VMEM((COLS + 2, 80, C), F32),
+            pltpu.VMEM((COLS + 2, ROWS, C), F32),
             pltpu.VMEM((4, PAIRS * ROWS, 3 * C), BF16),
             pltpu.VMEM((2,) + frame, BF16),
             pltpu.VMEM((2, 2, ROWS, C), BF16),
@@ -546,7 +558,15 @@
         tbias2.reshape(1, C),
         mix,
     )
-    return out.reshape(2, ROWS, COLS, C)
+    rows = pl.pallas_call(
+        untransposed,
+        grid=(8,),
+        out_shape=jax.ShapeDtypeStruct((2, POS, C), BF16),
+        in_specs=[pl.BlockSpec((1, PAIRS, 2, 16, C), lambda n: (n // 4, 0, 0, n % 4, 0))],
+        out_specs=pl.BlockSpec((1, HALF, C), lambda n: (n // 4, n % 4, 0)),
+        cost_estimate=pl.CostEstimate(flops=2**30, bytes_accessed=2**22, transcendentals=0),
+    )(out)
+    return rows.reshape(2, ROWS, COLS, C)
 
 
 def solution(mesh):

time: 102 us -> 84.8 us (0.83)
  Pallas kernels: 98.3 us -> 83.9 us
  local copies, waits for them, and re-layouts: 3.08 us -> 0 us
    pallas_call x1, Pallas kernels: 98.3 us -> 77.5 us  [body(): pl.pallas_call(functools.partial(kernel, nf, ns), out_shape=jax.ShapeDtyp...]
    pallas_call x0 -> x1, Pallas kernels: none -> 6.44 us  [body(): pl.pallas_call(untransposed, grid=(8,), out_shape=jax.ShapeDtypeStruct((2...]
    unnamed x1 -> x0, local copies, waits for them, and re-layouts: 3.08 us -> none
where the time goes in v2:
time: 84.8 us; the launch traced here: 84.6 us
  Pallas kernels  83.9 us (99%)
    pallas_call x1, Pallas kernels, body(): pl.pallas_call(functools.partial(kernel, nf, ns), out_shape=jax.ShapeDtyp...  77.5 us
    pallas_call x1, Pallas kernels, body(): pl.pallas_call(untransposed, grid=(8,), out_shape=jax.ShapeDtypeStruct((2...  6.44 us

profile of v2, /device:TPU:1, one launch (start us, length us, event | category | flops | bytes accessed | tf_op | source)
XLA Modules:
  0.0 84.6 jit_solution(10930321275908528078)
XLA Ops:
  0.7 77.5 %shard_map.136.x = bf16[2,8,2,64,512]{4,3,2,1,0:T(8,128)(2,1)} custom-call(bf16[2,1024,512]{2,1,0:T(8,128)(2,1)} %bitcast.6, f32[2,512]{1,0:T(2,128)} %norm1.1, bf16[3,3,512,512]{3,2,1,0:T(8,128)(2,1)} %conv1_hbm.1, f32[1,512]{1,0:T(1,128)} %bitcast.7, f32[2,512]{1,0:T(2,128)} %norm2.1, bf16[3,3,512,512]{3,2,1,0:T(8,128)(2,1)} %conv2_hbm.1, ...), custom_call_target="tpu_custom_call" | custom-call | flops 20000000000 | bytes 17825792 | tf_op jit(solution)/shard_map/pallas_call | solution.py:497
  78.1 6.4 %shard_map.137 = bf16[2,1024,512]{2,1,0:T(8,128)(2,1)} custom-call(bf16[2,8,2,64,512]{4,3,2,1,0:T(8,128)(2,1)} %shard_map.136.x), custom_call_target="tpu_custom_call" | custom-call | flops 1073741824 | bytes 4194304 | tf_op jit(solution)/shard_map/pallas_call | solution.py:561

commit v3 on v2

--- a/solution.py
+++ b/solution.py
@@ -265,16 +265,11 @@
     gather_wait(st1, 0)
 
     def spatial_stage(x, halo, fr, order, coef, u, finish):
-        @pl.loop(0, COLS, unroll=4)
-        def _(c):
-            s[c + 1] = act(x[fr, c // 2, lax.rem(c, 2)], coef)
-
-        s[0] = jnp.where(has_left, act(halo[order, 0], coef), 0.0)
-        s[COLS + 1] = jnp.where(has_right, act(halo[order, 1], coef), 0.0)
-
-        @pl.loop(0, PAIRS)
-        def _(p):
-            rows = pl.ds(pl.multiple_of(p * ROWS, ROWS), ROWS)
+        def column(c):
+            s[c + 1] = act(x[fr, c // 2, c % 2], coef)
+
+        def pair(p):
+            rows = slice(p * ROWS, (p + 1) * ROWS)
             top = lax.broadcasted_iota(jnp.int32, (ROWS, 128), 0) == 0
             bottom = lax.broadcasted_iota(jnp.int32, (ROWS, 128), 0) == ROWS - 1
             for q in range(4):
@@ -287,15 +282,28 @@
                     v[t, rows, C + lo : C + lo + 128] = part.astype(BF16)
                     v[t, rows, 2 * C + lo : 2 * C + lo + 128] = below.astype(BF16)
 
+        def products(h, n):
+            lanes = slice(n * HALF, (n + 1) * HALF)
+            rows = slice(h * HALF, (h + 1) * HALF)
+            return [jnp.dot(v[t, rows], u[t, :, lanes], preferred_element_type=F32) for t in range(4)]
+
+        s[0] = jnp.where(has_left, act(halo[order, 0], coef), 0.0)
+        s[COLS + 1] = jnp.where(has_right, act(halo[order, 1], coef), 0.0)
+        for c in range(10):
+            column(c)
+        for p in range(4):
+            pair(p)
+        early = [products(0, 0)]
+        for c in range(10, COLS):
+            column(c)
+        for p in range(4, 6):
+            pair(p)
+        early.append(products(0, 1))
+        for p in range(6, PAIRS):
+            pair(p)
         for n in range(2):
             lanes = slice(n * HALF, (n + 1) * HALF)
-            m = [
-                jnp.concatenate(
-                    [jnp.dot(v[t, h * HALF : (h + 1) * HALF], u[t, :, lanes], preferred_element_type=F32) for h in range(2)],
-                    axis=0,
-                )
-                for t in range(4)
-            ]
+            m = [jnp.concatenate(both, axis=0) for both in zip(early[n], products(1, n))]
             finish(n, lanes, m[0] + m[1] + m[2], m[1] - m[2] - m[3])
 
     def moments_of(parts):
@@ -383,44 +391,29 @@
         for n in range(2):
             to_peer(1, n, slice(n * HALF, (n + 1) * HALF)).start()
 
-    def fill(dst, src, coef):
-        @pl.loop(0, COLS, unroll=4)
-        def _(c):
-            dst[pl.ds(pl.multiple_of(c * ROWS, ROWS), ROWS), :] = act(src[c // 2, lax.rem(c, 2)], coef).astype(BF16)
-
-    fill(a3.at[2], sp.at[first_frame], coef3)
-    fill(a3.at[3], sp.at[second_frame], coef3)
+    def temporal_stage(fills, coef, products, tw, finish):
+        for h in range(POS // HALF):
+            for slot, src, kept in fills:
+                for c in range(4):
+                    value = act(src[2 * h + c // 2, c % 2], coef)
+                    if kept is not None:
+                        value = jnp.where(kept, value, 0.0)
+                    lo = h * HALF + c * ROWS
+                    a3[slot, lo : lo + ROWS, :] = value.astype(BF16)
+            rows = slice(h * HALF, (h + 1) * HALF)
+            for at in products:
+                taps = jnp.concatenate([a3[at - 1, rows], a3[at, rows], a3[at + 1, rows]], axis=1)
+                for n in range(2):
+                    lanes = slice(n * HALF, (n + 1) * HALF)
+                    finish(at, h, n, lanes, jnp.dot(taps, tw[:, lanes], preferred_element_type=F32))
+
     for copy in tw_loads:
         copy.wait()
-
-    def temporal(at, tw, lanes):
-        parts = []
-        for h in range(POS // HALF):
-            rows = slice(h * HALF, (h + 1) * HALF)
-            taps = jnp.concatenate([a3[at - 1, rows], a3[at, rows], a3[at + 1, rows]], axis=1)
-            parts.append(jnp.dot(taps, tw[:, lanes], preferred_element_type=F32))
-        return jnp.concatenate(parts, axis=0)
-
     for n in range(2):
         lanes = slice(n * HALF, (n + 1) * HALF)
         copy = to_partner(n, lanes)
         copy.wait_send()
         copy.wait_recv()
-    fill(a3.at[4], dd, coef3)
-
-    def tempo_frame(order, moments):
-        for n in range(2):
-            lanes = slice(n * HALF, (n + 1) * HALF)
-            values = temporal(1 + order, tw1, lanes) + tbias1[:, lanes]
-            tm[order, :, :, :, lanes] = values.reshape(PAIRS, 2, ROWS, HALF).astype(BF16)
-            if moments:
-                put_moments(st_own.at[7 + order], n * HALF, *moments_of([values]))
-
-    tempo_frame(2, True)
-    tempo_copy = pltpu.make_async_remote_copy(
-        tm.at[2], td, frame_send.at[3, 0], frame_recv.at[3, 0], device_id={"frame": partner}, device_id_type=MESH
-    )
-    tempo_copy.start()
 
     def peer_wait(order):
         @pl.when(has_peer)
@@ -430,45 +423,54 @@
                 copy.wait_send()
                 copy.wait_recv()
 
-    def fill_or_zero(dst, src, coef):
-        pl.when(has_peer)(lambda: fill(dst, src, coef))
-
-        @pl.when(jnp.logical_not(has_peer))
-        def _():
-            @pl.loop(0, COLS)
-            def _(c):
-                dst[pl.ds(pl.multiple_of(c * ROWS, ROWS), ROWS), :] = jnp.zeros((ROWS, C), BF16)
-
     peer_wait(0)
-    fill_or_zero(a3.at[1], near, coef3)
-    tempo_frame(1, True)
+    blocks = {}
+
+    def tempo_finish(at, h, n, lanes, product):
+        values = product + tbias1[:, lanes]
+        tm[at - 1, 2 * h : 2 * h + 2, :, :, lanes] = values.reshape(2, 2, ROWS, HALF).astype(BF16)
+        if at > 1:
+            blocks.setdefault((at, n), []).append(moments_of([values]))
+
+    temporal_stage(
+        [(2, sp.at[first_frame], None), (3, sp.at[second_frame], None), (4, dd, None), (1, near, has_peer)],
+        coef3, (3, 2), tw1, tempo_finish,
+    )
+    for (at, n), parts in blocks.items():
+        mean = sum(part[0] for part in parts) * (1.0 / len(parts))
+        square = sum(part[1] + float(HALF) * (part[0] - mean) * (part[0] - mean) for part in parts)
+        put_moments(st_own.at[6 + at], n * HALF, mean, square)
     span_first(8, 10, 5, st4s)
+    tempo_copy = pltpu.make_async_remote_copy(
+        tm.at[2], td, frame_send.at[3, 0], frame_recv.at[3, 0], device_id={"frame": partner}, device_id_type=MESH
+    )
+    tempo_copy.start()
     span_second(10, 5, st4s, 11, 6, st4f)
 
     peer_wait(1)
-    fill_or_zero(a3.at[0], far, coef3)
-    tempo_frame(0, False)
-
-    coef4 = span_done(11, 6, st4f, norm4)
-    fill(a3.at[2], tm.at[1], coef4)
-    fill(a3.at[3], tm.at[2], coef4)
-    fill_or_zero(a3.at[1], tm.at[0], coef4)
+    temporal_stage([(0, far, has_peer)], coef3, (1,), tw1, tempo_finish)
     tempo_copy.wait_send()
     tempo_copy.wait_recv()
-    fill(a3.at[4], td, coef4)
-
+
+    coef4 = span_done(11, 6, st4f, norm4)
     keep = 1.0 - 1.0 / (1.0 + jnp.exp(-jnp.full((1, HALF), mix[0], F32)))
     out_copies = []
-    for order, fr in ((0, first_frame), (1, second_frame)):
-        for n in range(2):
-            lanes = slice(n * HALF, (n + 1) * HALF)
-            branch = temporal(2 + order, tw2, lanes) + tbias2[:, lanes]
-            old = sp[fr, :, :, :, lanes].astype(F32).reshape(POS, HALF)
-            lx[fr, :, :, :, lanes] = (old + keep * branch).reshape(PAIRS, 2, ROWS, HALF).astype(BF16)
-
-        copy = pltpu.make_async_copy(lx.at[fr], out_hbm.at[fr], out_sem.at[order])
-        copy.start()
-        out_copies.append(copy)
+
+    def branch_finish(at, h, n, lanes, product):
+        fr = first_frame if at == 2 else second_frame
+        old = sp[fr, 2 * h : 2 * h + 2, :, :, lanes].astype(F32).reshape(HALF, HALF)
+        mixed = old + keep * (product + tbias2[:, lanes])
+        lx[fr, 2 * h : 2 * h + 2, :, :, lanes] = mixed.reshape(2, 2, ROWS, HALF).astype(BF16)
+        if n == 1:
+            part = pl.ds(2 * h, 2)
+            copy = pltpu.make_async_copy(lx.at[fr, part], out_hbm.at[fr, part], out_sem.at[at - 2, h])
+            copy.start()
+            out_copies.append(copy)
+
+    temporal_stage(
+        [(2, tm.at[1], None), (3, tm.at[2], None), (4, td, None), (1, tm.at[0], has_peer)],
+        coef4, (3, 2), tw2, branch_finish,
+    )
     for copy in out_copies:
         copy.wait()
 
@@ -479,9 +481,26 @@
     return jnp.where(i1 == (i0 & 15) * 16 + (i0 >> 4), 1.0, 0.0).astype(BF16)
 
 
-def untransposed(x, out):
-    moved = jnp.dot(transposition(), x[0].reshape(HALF, C), preferred_element_type=F32)
-    out[0] = moved.astype(BF16)
+def untransposed(x, out, taken, given, taken_sem, given_sem):
+    blocks = [(fr, b) for fr in range(2) for b in range(4)]
+    loads = [
+        pltpu.make_async_copy(x.at[fr, :, :, pl.ds(b * 16, 16), :], taken.at[n], taken_sem.at[n])
+        for n, (fr, b) in enumerate(blocks)
+    ]
+    stores = [
+        pltpu.make_async_copy(given.at[n], out.at[fr, pl.ds(b * HALF, HALF), :], given_sem.at[n])
+        for n, (fr, b) in enumerate(blocks)
+    ]
+    for load in loads:
+        load.start()
+    perm = transposition()
+    for n in range(8):
+        loads[n].wait()
+        moved = jnp.dot(perm, taken[n].reshape(HALF, C), preferred_element_type=F32)
+        given[n] = moved.astype(BF16)
+        stores[n].start()
+    for store in stores:
+        store.wait()
 
 
 def body(*args):
@@ -536,7 +555,7 @@
             pltpu.SemaphoreType.DMA((7,)),
             pltpu.SemaphoreType.DMA((4, 2)),
             pltpu.SemaphoreType.DMA((4, 2)),
-            pltpu.SemaphoreType.DMA((2,)),
+            pltpu.SemaphoreType.DMA((2, 4)),
         ],
         compiler_params=pltpu.CompilerParams(
             collective_id=0, has_side_effects=True, vmem_limit_bytes=62 * 2**20
@@ -560,10 +579,16 @@
     )
     rows = pl.pallas_call(
         untransposed,
-        grid=(8,),
         out_shape=jax.ShapeDtypeStruct((2, POS, C), BF16),
-        in_specs=[pl.BlockSpec((1, PAIRS, 2, 16, C), lambda n: (n // 4, 0, 0, n % 4, 0))],
-        out_specs=pl.BlockSpec((1, HALF, C), lambda n: (n // 4, n % 4, 0)),
+        in_specs=[hbm],
+        out_specs=hbm,
+        scratch_shapes=[
+            pltpu.VMEM((8, PAIRS, 2, 16, C), BF16),
+            pltpu.VMEM((8, HALF, C), BF16),
+            pltpu.SemaphoreType.DMA((8,)),
+            pltpu.SemaphoreType.DMA((8,)),
+        ],
+        compiler_params=pltpu.CompilerParams(vmem_limit_bytes=16 * 2**20),
         cost_estimate=pl.CostEstimate(flops=2**30, bytes_accessed=2**22, transcendentals=0),
     )(out)
     return rows.reshape(2, ROWS, COLS, C)

time: 84.8 us -> 77.6 us (0.915)
  Pallas kernels: 83.9 us -> 75 us
  local copies, waits for them, and re-layouts: 0 us -> 1.58 us
    pallas_call x1, Pallas kernels: 77.5 us -> 72.1 us  [body(): pl.pallas_call(functools.partial(kernel, nf, ns), out_shape=jax.ShapeDtyp...]
    pallas_call x1, Pallas kernels: 6.44 us -> 2.88 us  [body(): pl.pallas_call(untransposed, out_shape=jax.ShapeDtypeStruct((2, POS, C),...]
    unnamed x0 -> x2, local copies, waits for them, and re-layouts: none -> 1.58 us
where the time goes in v3:
time: 77.6 us; the launch traced here: 77.4 us
  Pallas kernels  75 us (97%)
  local copies, waits for them, and re-layouts  1.58 us (2%)
  between operations  0.85 us (1%)
    pallas_call x1, Pallas kernels, body(): pl.pallas_call(functools.partial(kernel, nf, ns), out_shape=jax.ShapeDtyp...  72.1 us
    pallas_call x1, Pallas kernels, body(): pl.pallas_call(untransposed, out_shape=jax.ShapeDtypeStruct((2, POS, C),...  2.88 us
    unnamed x2, local copies, waits for them, and re-layouts  1.58 us

profile of v3, /device:TPU:1, one launch (start us, length us, event | category | flops | bytes accessed | tf_op | source)
XLA Modules:
  0.0 77.4 jit_solution(14859256417602925780)
XLA Ops:
  0.7 72.1 %shard_map.136.x = bf16[2,8,2,64,512]{4,3,2,1,0:T(8,128)(2,1)} custom-call(bf16[2,1024,512]{2,1,0:T(8,128)(2,1)} %bitcast.6, f32[2,512]{1,0:T(2,128)} %norm1.1, bf16[3,3,512,512]{3,2,1,0:T(8,128)(2,1)} %conv1_hbm.1, f32[1,512]{1,0:T(1,128)} %bitcast.7, f32[2,512]{1,0:T(2,128)} %norm2.1, bf16[3,3,512,512]{3,2,1,0:T(8,128)(2,1)} %conv2_hbm.1, ...), custom_call_target="tpu_custom_call" | custom-call | flops 20000000000 | bytes 17825792 | tf_op jit(solution)/shard_map/pallas_call | solution.py:516
  72.8 0.0 copy-start
  72.8 1.6 %copy-done = bf16[2,8,2,64,512]{4,3,2,1,0:T(8,128)(2,1)S(1)} copy-done((bf16[2,8,2,64,512]{4,3,2,1,0:T(8,128)(2,1)S(1)}, bf16[2,8,2,64,512]{4,3,2,1,0:T(8,128)(2,1)}, u32[]{:S(2)}) %copy-start) | copy-done | bytes 2097176
  74.3 2.9 %shard_map.137 = bf16[2,1024,512]{2,1,0:T(8,128)(2,1)} custom-call(bf16[2,8,2,64,512]{4,3,2,1,0:T(8,128)(2,1)S(1)} %copy-done), custom_call_target="tpu_custom_call" | custom-call | flops 1073741824 | bytes 4194304 | tf_op jit(solution)/shard_map/pallas_call | solution.py:580
Async XLA Ops:
  72.8 1.6 %copy-start = (bf16[2,8,2,64,512]{4,3,2,1,0:T(8,128)(2,1)S(1)}, bf16[2,8,2,64,512]{4,3,2,1,0:T(8,128)(2,1)}, u32[]{:S(2)}) copy-start(bf16[2,8,2,64,512]{4,3,2,1,0:T(8,128)(2,1)} %shard_map.136.x) | copy-start | bytes 6291460

commit v4 on v3

--- a/solution.py
+++ b/solution.py
@@ -588,7 +588,7 @@
             pltpu.SemaphoreType.DMA((8,)),
             pltpu.SemaphoreType.DMA((8,)),
         ],
-        compiler_params=pltpu.CompilerParams(vmem_limit_bytes=16 * 2**20),
+        compiler_params=pltpu.CompilerParams(vmem_limit_bytes=62 * 2**20),
         cost_estimate=pl.CostEstimate(flops=2**30, bytes_accessed=2**22, transcendentals=0),
     )(out)
     return rows.reshape(2, ROWS, COLS, C)

time: 77.6 us -> 76.7 us (0.988)
  local copies, waits for them, and re-layouts: 1.58 us -> 0 us
    unnamed x2 -> x0, local copies, waits for them, and re-layouts: 1.58 us -> none
where the time goes in v4:
time: 76.7 us; the launch traced here: 76.6 us
  Pallas kernels  75.7 us (99%)
  between operations  0.84 us (1%)
    pallas_call x1, Pallas kernels, body(): pl.pallas_call(functools.partial(kernel, nf, ns), out_shape=jax.ShapeDtyp...  72.1 us
    pallas_call x1, Pallas kernels, body(): pl.pallas_call(untransposed, out_shape=jax.ShapeDtypeStruct((2, POS, C),...  3.64 us

profile of v4, /device:TPU:1, one launch (start us, length us, event | category | flops | bytes accessed | tf_op | source)
XLA Modules:
  0.0 76.6 jit_solution(5172126558253862183)
XLA Ops:
  0.7 72.1 %shard_map.136.x = bf16[2,8,2,64,512]{4,3,2,1,0:T(8,128)(2,1)} custom-call(bf16[2,1024,512]{2,1,0:T(8,128)(2,1)} %bitcast.6, f32[2,512]{1,0:T(2,128)} %norm1.1, bf16[3,3,512,512]{3,2,1,0:T(8,128)(2,1)} %conv1_hbm.1, f32[1,512]{1,0:T(1,128)} %bitcast.7, f32[2,512]{1,0:T(2,128)} %norm2.1, bf16[3,3,512,512]{3,2,1,0:T(8,128)(2,1)} %conv2_hbm.1, ...), custom_call_target="tpu_custom_call" | custom-call | flops 20000000000 | bytes 17825792 | tf_op jit(solution)/shard_map/pallas_call | solution.py:516
  72.8 3.6 %shard_map.137 = bf16[2,1024,512]{2,1,0:T(8,128)(2,1)} custom-call(bf16[2,8,2,64,512]{4,3,2,1,0:T(8,128)(2,1)} %shard_map.136.x), custom_call_target="tpu_custom_call" | custom-call | flops 1073741824 | bytes 4194304 | tf_op jit(solution)/shard_map/pallas_call | solution.py:580
